TPU v7x, 32 devices: a whole 2x2x4 slice. The times are simulated.
32 devices in a mesh: seq: 4 (over y, core), buf: 8 (over z, x).
Axes of the slice: x: 2, y: 2, z: 4, core: 2. Of those that a mesh axis runs over, the one named last changes fastest.
Arguments:
- row_inputs: bfloat16 [64, 128, 1024], P(('seq', 'buf')), may hold values from -6 to 6
- row_shared: bfloat16 [64, 128, 128], P(('seq', 'buf')), may hold values from -4 to 4
- row_steps: bfloat16 [64, 128, 16], P(('seq', 'buf')), may hold values from -3 to 3
- row_count: int32 [32], P(('seq', 'buf')), may hold values from 0 to 2, as said below
- row_slot: int32 [64], P(('seq', 'buf')), may hold values from 0 to 47, as said below
- doc_start: int32 [6144], P('seq'), may hold values from 0 to 1, as said below
- decay_log: float32 [16], P('buf'), may hold values from -9.2 to 2.78
- step_bias: float32 [16], P('buf'), may hold values from -6.92 to -3.89
- skip_gain: float32 [16], P('buf'), may hold values from 0.5 to 1.5
Outputs:
- mixer_out: bfloat16 [6144, 1024], P('seq', 'buf')
Inputs may be any that keep to these rules, and one draw needn't show every extreme that they name: `row_count`: over the 8 hosts of one sequence shard the counts sum to 12; in every shard some host holds 2 live buffers. `row_slot`: A live buffer's stream row lies in its host's own sequence shard (rows 12 * s to 12 * s + 11 for shard s), and the live buffers of a shard fill each of its rows exactly once; entries of buffers that are not live are arbitrary rows of the same shard. `doc_start`: there are max(1, 1) ones, one in each of as many consecutive sequence shards.
All inputs are finite; a program needn't handle non-finite values.
Results may differ from a plain program's by a relative error of at most 0.0065.
Values may be sent and summed in bfloat16 or wider, within the bound.
A program may use at most 64 MiB of HBM per device.

v0:
```python
from functools import partial

import jax
import jax.numpy as jnp
from jax import lax
from jax.sharding import PartitionSpec as P

SPAN = 256


def from_behind(array, axis, by):
    devices = lax.axis_size(axis)
    pairs = [(i, i + by) for i in range(devices) if 0 <= i + by < devices]
    return lax.ppermute(array, axis, pairs)


def span_parts(inputs, shared, raw_steps, starts, decay_log, step_bias):
    length = inputs.shape[0]
    state_size = shared.shape[1] // 2
    b_part = shared[:, :state_size]
    c_part = shared[:, state_size:]
    step_size = jax.nn.softplus(raw_steps.astype(jnp.float32) + step_bias)
    log_decay = -step_size * jnp.exp(decay_log)
    decay_sum = jnp.cumsum(log_decay, axis=0)
    reset_count = jnp.cumsum(starts, axis=0)
    scores = jnp.einsum("tn,sn->ts", c_part, b_part, preferred_element_type=jnp.float32)
    position = jnp.arange(length, dtype=jnp.int32)
    together = (reset_count[:, None] == reset_count[None, :]) & (
        position[:, None] >= position[None, :]
    )
    gap_sum = decay_sum.T[:, :, None] - decay_sum.T[:, None, :]
    factor = jnp.where(together[None], jnp.exp(jnp.where(together[None], gap_sum, 0.0)), 0.0)
    weight = (scores[None] * factor * step_size.T[:, None, :]).astype(jnp.bfloat16)
    within_span = jnp.einsum("hts,shp->thp", weight, inputs, preferred_element_type=jnp.float32)
    keep_tail = reset_count == reset_count[-1]
    tail_factor = (
        jnp.where(keep_tail[:, None], jnp.exp(decay_sum[-1][None, :] - decay_sum), 0.0) * step_size
    )
    weighted = (inputs.astype(jnp.float32) * tail_factor[:, :, None]).astype(jnp.bfloat16)
    span_state = jnp.einsum("shp,sn->hpn", weighted, b_part, preferred_element_type=jnp.float32)
    entry_scale = jnp.where((reset_count == 0)[:, None], jnp.exp(decay_sum), 0.0)
    return (within_span, span_state, decay_sum[-1], reset_count[-1], entry_scale)


def per_device(
    row_inputs,
    row_shared,
    row_steps,
    row_count,
    row_slot,
    doc_start,
    decay_log,
    step_bias,
    skip_gain,
):
    groups = lax.axis_size("buf")
    buffers, row_len, inner = row_inputs.shape
    heads_dev = decay_log.shape[0]
    head_size = inner // (groups * heads_dev)
    state_cols = row_shared.shape[2]
    state_size = state_cols // 2
    tokens = doc_start.shape[0]
    stream_rows = tokens // row_len
    pieces = row_inputs.reshape(buffers, row_len, groups, heads_dev * head_size)
    step_pieces = row_steps.reshape(buffers, row_len, groups, heads_dev)
    tiled = jnp.broadcast_to(row_shared[:, :, None, :], (buffers, row_len, groups, state_cols))
    got_inputs, got_steps, got_shared = (
        lax.all_to_all(pieces, "buf", split_axis=2, concat_axis=0, tiled=True),
        lax.all_to_all(step_pieces, "buf", split_axis=2, concat_axis=0, tiled=True),
        lax.all_to_all(tiled, "buf", split_axis=2, concat_axis=0, tiled=True),
    )
    got_shared = got_shared.reshape(groups * buffers, row_len, state_cols)
    all_slots, all_counts = (
        lax.all_gather(row_slot, "buf", axis=0, tiled=True),
        lax.all_gather(row_count, "buf", axis=0, tiled=True),
    )
    buffer_index = jnp.arange(groups * buffers, dtype=jnp.int32)
    is_live = buffer_index % buffers < jnp.repeat(all_counts, buffers)
    local_slot = all_slots - lax.axis_index("seq") * stream_rows
    target = jnp.where(is_live, local_slot, stream_rows)
    source = jnp.zeros((stream_rows,), jnp.int32).at[target].set(buffer_index, mode="drop")
    spans = tokens // SPAN
    inputs = got_inputs.reshape(groups * buffers, row_len, heads_dev * head_size)[source]
    inputs = inputs.reshape(spans, SPAN, heads_dev, head_size)
    shared = got_shared[source].reshape(spans, SPAN, state_cols)
    raw_steps = got_steps.reshape(groups * buffers, row_len, heads_dev)[source].reshape(
        spans, SPAN, heads_dev
    )
    starts = doc_start.reshape(spans, SPAN)
    per_block = 2
    while spans % (2 * per_block) == 0 and spans // per_block > 16:
        per_block = 2 * per_block
    blocks = spans // per_block

    def span_block(block_parts):
        return jax.vmap(partial(span_parts, decay_log=decay_log, step_bias=step_bias))(*block_parts)

    def blocked(array):
        return array.reshape((blocks, per_block) + array.shape[1:])

    def unblocked(array):
        return array.reshape((spans,) + array.shape[2:])

    results = lax.map(
        span_block, (blocked(inputs), blocked(shared), blocked(raw_steps), blocked(starts))
    )
    within_span, span_state, tail_sum, tail_reset, entry_scale = [
        unblocked(result_part) for result_part in results
    ]
    shard_sum = jnp.cumsum(tail_sum, axis=0)
    shard_resets = jnp.cumsum(tail_reset, axis=0)
    prior_sum = jnp.concatenate([jnp.zeros((1, heads_dev), jnp.float32), shard_sum[:-1]], axis=0)
    prior_resets = jnp.concatenate([jnp.zeros((1,), shard_resets.dtype), shard_resets[:-1]], axis=0)
    span_order = jnp.arange(spans, dtype=jnp.int32)
    reachable = (span_order[None, :] < span_order[:, None]) & (
        prior_resets[:, None] == shard_resets[None, :]
    )
    gap_sum = prior_sum.T[:, :, None] - shard_sum.T[:, None, :]
    carry_matrix = jnp.where(
        reachable[None], jnp.exp(jnp.where(reachable[None], gap_sum, 0.0)), 0.0
    )
    local_in = jnp.einsum(
        "hck,khpn->chpn", carry_matrix, span_state, precision=lax.Precision.HIGHEST
    )
    enter_scale = jnp.where((prior_resets == 0)[:, None], jnp.exp(prior_sum), 0.0)
    last_keep = shard_resets == shard_resets[-1]
    leave_scale = jnp.where(last_keep[:, None], jnp.exp(shard_sum[-1][None, :] - shard_sum), 0.0)
    summary = jnp.einsum("kh,khpn->hpn", leave_scale, span_state, precision=lax.Precision.HIGHEST)
    shard_pass = jnp.where(shard_resets[-1] == 0, jnp.exp(shard_sum[-1]), 0.0)
    empty_state = jnp.zeros((heads_dev, head_size, state_size), jnp.float32)

    def handoff(handoff_step, entering_now):
        leaving = shard_pass[:, None, None] * entering_now + summary
        return from_behind(leaving.astype(jnp.bfloat16), "seq", 1).astype(leaving.dtype)

    entering = lax.fori_loop(0, lax.axis_size("seq") - 1, handoff, empty_state)
    incoming = local_in + enter_scale[:, :, None, None] * entering[None]
    carried = incoming.astype(jnp.bfloat16)
    c_part = shared[:, :, state_size:]
    from_state = jnp.einsum("ctn,chpn->cthp", c_part, carried, preferred_element_type=jnp.float32)
    mixed = (
        within_span
        + from_state * entry_scale[:, :, :, None]
        + skip_gain[None, None, :, None] * inputs.astype(jnp.float32)
    )
    return mixed.astype(jnp.bfloat16).reshape(tokens, heads_dev * head_size)


def solution(mesh):
    return jax.shard_map(
        per_device,
        mesh=mesh,
        in_specs=(
            P(("seq", "buf"), None, None),
            P(("seq", "buf"), None, None),
            P(("seq", "buf"), None, None),
            P(("seq", "buf")),
            P(("seq", "buf")),
            P("seq"),
            P("buf"),
            P("buf"),
            P("buf"),
        ),
        out_specs=P("seq", "buf"),
        check_vma=False,
    )
```

profile of v0, /device:TPU:1, one launch (start us, length us, event | category | flops | bytes accessed | tf_op | source)
XLA Modules:
  0.0 94.4 jit_solution(13402242311050254016)
XLA Ops:
  0.0 1.3 %copy.116 = bf16[2,128,16]{1,0,2:T(2,128)(2,1)} copy(bf16[2,128,16]{1,2,0:T(8,128)(2,1)} %param.15) | data formatting | bytes 16384 | tf_op args[2]
  1.3 6.4 %all-to-all-start.2 = ((bf16[2,128,8,2]{1,0,3,2:T(2,128)(2,1)}), bf16[2,128,8,2]{1,0,3,2:T(2,128)(2,1)S(1)}, u32[]{:S(2)}, u32[]{:S(2)}) async-start(bf16[2,128,8,2]{1,0,3,2:T(2,128)(2,1)} %bitcast.25), calls=%async_computation.2 | async-start | bytes 16384 | tf_op jit(solution)/shard_map/all_to_all | solution.py:69
  7.7 1.3 %copy.112 = bf16[2,128,1024]{1,2,0:T(8,128)(2,1)S(1)} copy(bf16[2,128,1024]{2,1,0:T(8,128)(2,1)} %param.13) | data formatting | bytes 1048576 | tf_op args[0]
  9.1 3.9 %all-to-all-done.2 = bf16[2,128,8,2]{1,0,3,2:T(2,128)(2,1)S(1)} async-done(((bf16[2,128,8,2]{1,0,3,2:T(2,128)(2,1)}), bf16[2,128,8,2]{1,0,3,2:T(2,128)(2,1)S(1)}, u32[]{:S(2)}, u32[]{:S(2)}) %all-to-all-start.2) | async-done | bytes 8224 | tf_op jit(solution)/shard_map/all_to_all | solution.py:69
  13.0 15.8 %all_to_all.45 = bf16[2,128,8,128]{1,3,0,2:T(8,128)(2,1)S(1)} all-to-all(bf16[2,128,8,128]{1,3,0,2:T(8,128)(2,1)S(1)} %copy.113), channel_id=1, replica_groups=mesh['seq'=4,'buf'=8] {'buf'}, dimensions={2} | all-to-all | bytes 1048576 | tf_op jit(solution)/shard_map/all_to_all | solution.py:68
  28.8 0.9 broadcast_in_dim.181
  29.7 4.3 %all-to-all-start.1 = ((bf16[2,128,8,128]{3,1,0,2:T(8,128)(2,1)}), bf16[2,128,8,128]{3,1,0,2:T(8,128)(2,1)S(1)}, u32[]{:S(2)}, u32[]{:S(2)}) async-start(bf16[2,128,8,128]{3,1,0,2:T(8,128)(2,1)} %broadcast_in_dim.181), calls=%async_computation.1 | async-start | bytes 1048576 | tf_op jit(solution)/shard_map/all_to_all | solution.py:70
  35.9 0.8 dynamic-update-slice
  36.9 10.5 %all-reduce.3 = (s32[16]{0:T(128)S(1)}, s32[8]{0:T(128)S(1)}) all-reduce(s32[16]{0:T(128)S(1)} %dynamic-update-slice.1, s32[8]{0:T(128)S(1)} %dynamic-update-slice), channel_id=1, replica_groups=mesh['seq'=4,'buf'=8] {'buf'}, use_global_device_ids=true, to_apply=%add.2 | all-reduce | flops 24 | bytes 192
  49.1 0.6 gather_fusion
  49.8 0.6 gather_fusion.1
  51.2 16.9 %while.31 = (s32[]{:T(128)}, f32[3,2,256,2,64]{2,4,3,1,0:T(8,128)}, f32[3,2,2,64,64]{4,3,2,1,0:T(8,128)S(1)}, f32[3,2,2]{2,1,0:T(2,128)S(1)}, s32[3,2]{1,0:T(4,1...) while((s32[]{:T(128)}, f32[3,2,256,2,64]{2,4,3,1,0:T(8,128)}, ...), condition=%wide.region_6.7_spmd, body=%wide.region_1.6_spmd.sunk | while | flops 61029392 | bytes 2929725 | solution.py:104
  51.3 0.6 reduce-window.40
  52.8 1.2 %reduce-window.38 = f32[2,2,2,128]{3,2,1,0:T(2,128)S(1)} reduce-window(f32[2,2,2,128]{3,2,1,0:T(2,128)S(1)} %reshape.359, f32[]{:T(128)} %constant.89.clone.1..sunk), window={size=1x1x1x128 pad=0_0x0_0x0_0x127_0}, to_apply=%region_4.4 | reduce-window | flops 130048 | bytes 8196 | tf_op jit(solution)/shard_map/reduce-window.11
  55.7 1.2 %fusion.65 = f32[3,2,256,2,64]{2,4,3,1,0:T(8,128)} fusion(f32[3,2,256,2,64]{2,4,3,1,0:T(8,128)} %get-tuple-element.412, s32[]{:T(128)S(6)} %copy.180, f32[2,2,256]{2,1,0:T(2,128)S(1)} %bitcast.167, f32[2,2,256]{2,1,0:T(2,128)S(1)} %reduce_window_sum.94, f32[2,256,256]{2,1,0:T(8,128)S(1)} %fusion.64, pred[2,256,256]{2,1,0:T(8,128)(4,1)S(1)} %compare_and_fusion.2, ...), kind=kOutput, calls=%fused_computation.8.clone.1 | convolution fusion | flops 35127296 | bytes 1061888 | tf_op jit(solution)/shard_map/while/body/eval_jaxpr/vmap(hts,shp->thp)/dot_general | solution.py:34
  58.4 1.2 %reduce-window.38 = f32[2,2,2,128]{3,2,1,0:T(2,128)S(1)} reduce-window(f32[2,2,2,128]{3,2,1,0:T(2,128)S(1)} %reshape.359, f32[]{:T(128)} %constant.89.clone.1..sunk), window={size=1x1x1x128 pad=0_0x0_0x0_0x127_0}, to_apply=%region_4.4 | reduce-window | flops 130048 | bytes 8196 | tf_op jit(solution)/shard_map/reduce-window.11
  61.3 1.2 %fusion.65 = f32[3,2,256,2,64]{2,4,3,1,0:T(8,128)} fusion(f32[3,2,256,2,64]{2,4,3,1,0:T(8,128)} %get-tuple-element.412, s32[]{:T(128)S(6)} %copy.180, f32[2,2,256]{2,1,0:T(2,128)S(1)} %bitcast.167, f32[2,2,256]{2,1,0:T(2,128)S(1)} %reduce_window_sum.94, f32[2,256,256]{2,1,0:T(8,128)S(1)} %fusion.64, pred[2,256,256]{2,1,0:T(8,128)(4,1)S(1)} %compare_and_fusion.2, ...), kind=kOutput, calls=%fused_computation.8.clone.1 | convolution fusion | flops 35127296 | bytes 1061888 | tf_op jit(solution)/shard_map/while/body/eval_jaxpr/vmap(hts,shp->thp)/dot_general | solution.py:34
  64.0 1.2 %reduce-window.38 = f32[2,2,2,128]{3,2,1,0:T(2,128)S(1)} reduce-window(f32[2,2,2,128]{3,2,1,0:T(2,128)S(1)} %reshape.359, f32[]{:T(128)} %constant.89.clone.1..sunk), window={size=1x1x1x128 pad=0_0x0_0x0_0x127_0}, to_apply=%region_4.4 | reduce-window | flops 130048 | bytes 8196 | tf_op jit(solution)/shard_map/reduce-window.11
  66.9 1.2 %fusion.65 = f32[3,2,256,2,64]{2,4,3,1,0:T(8,128)} fusion(f32[3,2,256,2,64]{2,4,3,1,0:T(8,128)} %get-tuple-element.412, s32[]{:T(128)S(6)} %copy.180, f32[2,2,256]{2,1,0:T(2,128)S(1)} %bitcast.167, f32[2,2,256]{2,1,0:T(2,128)S(1)} %reduce_window_sum.94, f32[2,256,256]{2,1,0:T(8,128)S(1)} %fusion.64, pred[2,256,256]{2,1,0:T(8,128)(4,1)S(1)} %compare_and_fusion.2, ...), kind=kOutput, calls=%fused_computation.8.clone.1 | convolution fusion | flops 35127296 | bytes 1061888 | tf_op jit(solution)/shard_map/while/body/eval_jaxpr/vmap(hts,shp->thp)/dot_general | solution.py:34
  69.7 0.7 broadcast_compare_fusion.2
  70.5 0.9 reshape.348
  71.9 0.7 copy.128
  72.8 0.8 fusion.34
  73.6 18.0 %while.32 = (s32[]{:T(128)}, f32[2,64,64]{2,1,0:T(8,128)S(1)}, f32[2]{0:T(128)S(1)}, f32[2,64,64]{2,1,0:T(8,128)S(1)}, s32[]{:T(128)}, /*index=5*/s32[]{:T(128)}) while((s32[]{:T(128)}, f32[2,64,64]{2,1,0:T(8,128)S(1)}, f32[2]{0:T(128)S(1)}, f32[2,64,64]{2,1,0:T(8,128)S(1)}, s32[]{:T(128)}, /*index=5*/s32[]{:T(128)}) %tuple.62), condition=%wide.region_10.11_spmd.clone, body=%wide.region_9.10_spmd.clone.sunk | while | flops 40963 | bytes 196735 | solution.py:136
  73.7 6.2 %collective-permute-start = (bf16[2,64,64]{2,1,0:T(8,128)(2,1)S(1)}, bf16[2,64,64]{2,1,0:T(8,128)(2,1)S(1)}, u32[]{:S(2)}, u32[]{:S(2)}) collective-permute-start(bf16[2,64,64]{2,1,0:T(8,128)(2,1)S(1)} %fusion.67), channel_id=1, source_target_pairs={{0,8},{8,16},{16,24},{1,9},{9,17},{17,25},{2,10},{10,18},{18,26},{... | collective-permute-start | bytes 49160 | tf_op jit(solution)/shard_map/while/body/eval_jaxpr/ppermute | solution.py:14
  79.9 1.0 %collective-permute-done = bf16[2,64,64]{2,1,0:T(8,128)(2,1)S(1)} collective-permute-done((bf16[2,64,64]{2,1,0:T(8,128)(2,1)S(1)}, bf16[2,64,64]{2,1,0:T(8,128)(2,1)S(1)}, u32[]{:S(2)}, u32[]{:S(2)}) %collective-permute-start) | collective-permute-done | bytes 16416 | tf_op jit(solution)/shard_map/while/body/eval_jaxpr/ppermute | solution.py:14
  81.0 4.2 %collective-permute-start = (bf16[2,64,64]{2,1,0:T(8,128)(2,1)S(1)}, bf16[2,64,64]{2,1,0:T(8,128)(2,1)S(1)}, u32[]{:S(2)}, u32[]{:S(2)}) collective-permute-start(bf16[2,64,64]{2,1,0:T(8,128)(2,1)S(1)} %fusion.67), channel_id=1, source_target_pairs={{0,8},{8,16},{16,24},{1,9},{9,17},{17,25},{2,10},{10,18},{18,26},{... | collective-permute-start | bytes 49160 | tf_op jit(solution)/shard_map/while/body/eval_jaxpr/ppermute | solution.py:14
  85.2 1.0 %collective-permute-done = bf16[2,64,64]{2,1,0:T(8,128)(2,1)S(1)} collective-permute-done((bf16[2,64,64]{2,1,0:T(8,128)(2,1)S(1)}, bf16[2,64,64]{2,1,0:T(8,128)(2,1)S(1)}, u32[]{:S(2)}, u32[]{:S(2)}) %collective-permute-start) | collective-permute-done | bytes 16416 | tf_op jit(solution)/shard_map/while/body/eval_jaxpr/ppermute | solution.py:14
  86.3 4.2 %collective-permute-start = (bf16[2,64,64]{2,1,0:T(8,128)(2,1)S(1)}, bf16[2,64,64]{2,1,0:T(8,128)(2,1)S(1)}, u32[]{:S(2)}, u32[]{:S(2)}) collective-permute-start(bf16[2,64,64]{2,1,0:T(8,128)(2,1)S(1)} %fusion.67), channel_id=1, source_target_pairs={{0,8},{8,16},{16,24},{1,9},{9,17},{17,25},{2,10},{10,18},{18,26},{... | collective-permute-start | bytes 49160 | tf_op jit(solution)/shard_map/while/body/eval_jaxpr/ppermute | solution.py:14
  90.6 1.0 %collective-permute-done = bf16[2,64,64]{2,1,0:T(8,128)(2,1)S(1)} collective-permute-done((bf16[2,64,64]{2,1,0:T(8,128)(2,1)S(1)}, bf16[2,64,64]{2,1,0:T(8,128)(2,1)S(1)}, u32[]{:S(2)}, u32[]{:S(2)}) %collective-permute-start) | collective-permute-done | bytes 16416 | tf_op jit(solution)/shard_map/while/body/eval_jaxpr/ppermute | solution.py:14
  91.6 0.8 fusion.33
  93.3 1.1 %reshape.349 = bf16[1536,128]{1,0:T(8,128)(2,1)} reshape(bf16[6,256,2,64]{3,2,1,0:T(2,128)(2,1)S(1)} %copy.141) | data formatting | bytes 786432 | tf_op jit(solution)/shard_map/reshape | solution.py:146
  (145 shorter events, 15.0 us)
Async XLA Ops:
  1.3 11.7 %all-to-all-start.2 = ((bf16[2,128,8,2]{1,0,3,2:T(2,128)(2,1)}), bf16[2,128,8,2]{1,0,3,2:T(2,128)(2,1)S(1)}, u32[]{:S(2)}, u32[]{:S(2)}) async-start(bf16[2,128,8,2]{1,0,3,2:T(2,128)(2,1)} %bitcast.25), calls=%async_computation.2 | async-start | bytes 16384 | tf_op jit(solution)/shard_map/all_to_all | solution.py:69
  7.7 21.1 %copy-start.1 = (bf16[2,128,128]{2,1,0:T(8,128)(2,1)S(1)}, bf16[2,128,128]{2,1,0:T(8,128)(2,1)}, u32[]{:S(2)}) copy-start(bf16[2,128,128]{2,1,0:T(8,128)(2,1)} %param.14) | copy-start | bytes 196612
  9.1 25.5 %copy-start.7 = (u32[32]{0:T(128)S(1)}, u32[32]{0:T(128)}, u32[]{:S(2)}) copy-start(u32[32]{0:T(128)} %constant.108) | copy-start | bytes 388
  9.1 27.5 %copy-start.5 = (s32[2]{0:T(128)S(1)}, s32[2]{0:T(128)}, u32[]{:S(2)}) copy-start(s32[2]{0:T(128)} %param.17) | copy-start | bytes 28
  9.1 38.4 %copy-start.3 = (s32[1536]{0:T(1024)S(1)}, s32[1536]{0:T(1024)}, u32[]{:S(2)}) copy-start(s32[1536]{0:T(1024)} %param.18) | copy-start | bytes 18436
  9.1 39.1 %copy-start.6 = (f32[2]{0:T(128)S(1)}, f32[2]{0:T(128)}, u32[]{:S(2)}) copy-start(f32[2]{0:T(128)} %param.19) | copy-start | bytes 28
  29.7 20.1 %all-to-all-start.1 = ((bf16[2,128,8,128]{3,1,0,2:T(8,128)(2,1)}), bf16[2,128,8,128]{3,1,0,2:T(8,128)(2,1)S(1)}, u32[]{:S(2)}, u32[]{:S(2)}) async-start(bf16[2,128,8,128]{3,1,0,2:T(8,128)(2,1)} %broadcast_in_dim.181), calls=%async_computation.1 | async-start | bytes 1048576 | tf_op jit(solution)/shard_map/all_to_all | solution.py:70
  49.8 1.5 %copy-start.2 = (f32[2]{0:T(128)S(1)}, f32[2]{0:T(128)}, u32[]{:S(2)}) copy-start(f32[2]{0:T(128)} %param.20) | copy-start | bytes 28
  72.7 19.7 %copy-start = (f32[3,2,256,2,64]{2,4,3,1,0:T(8,128)S(1)}, f32[3,2,256,2,64]{2,4,3,1,0:T(8,128)}, u32[]{:S(2)}) copy-start(f32[3,2,256,2,64]{2,4,3,1,0:T(8,128)} %get-tuple-element.169) | copy-start | bytes 2359300
  72.7 19.7 %copy-start.4 = (f32[2]{0:T(128)S(1)}, f32[2]{0:T(128)}, u32[]{:S(2)}) copy-start(f32[2]{0:T(128)} %param.21) | copy-start | bytes 28
  73.7 7.2 %collective-permute-start = (bf16[2,64,64]{2,1,0:T(8,128)(2,1)S(1)}, bf16[2,64,64]{2,1,0:T(8,128)(2,1)S(1)}, u32[]{:S(2)}, u32[]{:S(2)}) collective-permute-start(bf16[2,64,64]{2,1,0:T(8,128)(2,1)S(1)} %fusion.67), channel_id=1, source_target_pairs={{0,8},{8,16},{16,24},{1,9},{9,17},{17,25},{2,10},{10,18},{18,26},{... | collective-permute-start | bytes 49160 | tf_op jit(solution)/shard_map/while/body/eval_jaxpr/ppermute | solution.py:14
  81.0 5.2 %collective-permute-start = (bf16[2,64,64]{2,1,0:T(8,128)(2,1)S(1)}, bf16[2,64,64]{2,1,0:T(8,128)(2,1)S(1)}, u32[]{:S(2)}, u32[]{:S(2)}) collective-permute-start(bf16[2,64,64]{2,1,0:T(8,128)(2,1)S(1)} %fusion.67), channel_id=1, source_target_pairs={{0,8},{8,16},{16,24},{1,9},{9,17},{17,25},{2,10},{10,18},{18,26},{... | collective-permute-start | bytes 49160 | tf_op jit(solution)/shard_map/while/body/eval_jaxpr/ppermute | solution.py:14
  86.3 5.2 %collective-permute-start = (bf16[2,64,64]{2,1,0:T(8,128)(2,1)S(1)}, bf16[2,64,64]{2,1,0:T(8,128)(2,1)S(1)}, u32[]{:S(2)}, u32[]{:S(2)}) collective-permute-start(bf16[2,64,64]{2,1,0:T(8,128)(2,1)S(1)} %fusion.67), channel_id=1, source_target_pairs={{0,8},{8,16},{16,24},{1,9},{9,17},{17,25},{2,10},{10,18},{18,26},{... | collective-permute-start | bytes 49160 | tf_op jit(solution)/shard_map/while/body/eval_jaxpr/ppermute | solution.py:14
where the time goes:
time: 94.9 us; the launch traced here: 94.4 us
  blocking collectives  26.2 us (28%)
  starting transfers between devices  25.3 us (27%)
  local copies, waits for them, and re-layouts  16 us (17%)
  other arithmetic  10.6 us (11%)
  waiting for transfers between devices  6.92 us (7%)
  matrix products  6.89 us (7%)
  between operations  2.28 us (2%)
    all_to_all x1, blocking collectives, per_device(): lax.all_to_all(pieces, 'buf', split_axis=2, concat_axis=0, tiled=True)  15.8 us
    ppermute x3, starting transfers between devices, from_behind(): return lax.ppermute(array, axis, pairs)  14.6 us
    unnamed x1, blocking collectives  10.5 us
    another operation x21, other arithmetic  7.78 us
    all_to_all x1, starting transfers between devices, per_device(): lax.all_to_all(step_pieces, 'buf', split_axis=2, concat_axis=0, tiled=True)  6.35 us
    unnamed x22, local copies, waits for them, and re-layouts  4.27 us
    all_to_all x1, starting transfers between devices, per_device(): lax.all_to_all(tiled, 'buf', split_axis=2, concat_axis=0, tiled=True)  4.26 us
    all_to_all x1, waiting for transfers between devices, per_device(): lax.all_to_all(step_pieces, 'buf', split_axis=2, concat_axis=0, tiled=True)  3.91 us
  transfers between devices with their start and end apart: 5, of which 4 were waited for; matrix products, arithmetic and copies ran while one was open for 6% of the time, Pallas kernels for 0%

commit v1 on v0

v1 whole, which is shorter than its diff:
```python
import functools

import jax
import jax.numpy as jnp
from jax import lax
from jax.experimental import pallas as pl
from jax.experimental.pallas import tpu as pltpu
from jax.sharding import PartitionSpec as P

MESH = pl.DeviceIdType.MESH
EXACT = lax.Precision.HIGHEST


def softplus(value):
    small = jnp.exp(-jnp.abs(value))
    ratio = small / (small + 2.0)
    square = ratio * ratio
    series = jnp.full_like(ratio, 1.0 / 17.0)
    for odd in (15.0, 13.0, 11.0, 9.0, 7.0, 5.0, 3.0, 1.0):
        series = series * square + 1.0 / odd
    return jnp.maximum(value, 0.0) + 2.0 * ratio * series


def kernel(
    n, ns, heads_dev, stream_rows,
    inputs_ref, shared_ref, steps_ref, count_ref, slot_ref, doc_ref, log_ref, bias_ref, gain_ref,
    out_ref,
    xbuf, sbuf, step_out, step_in, meta_out, meta_in, meta_smem, source,
    docs, cums, counts_in, steps_q, enters, tails, passes,
    ybuf, ebuf, span_state, row_pass, incoming, prior_pass, leave_out, leave_in,
    x_send, x_recv, s_send, s_recv, f_send, st_send, st_recv, m_send, m_recv, l_send, l_recv, own_sem,
):
    me = lax.axis_index("buf")
    sq = lax.axis_index("seq")
    bit = lax.rem(me, 2)
    partner = me + 1 - 2 * bit
    buffers, row_len = steps_ref.shape[0], steps_ref.shape[1]
    width = xbuf.shape[3]
    head_size = width // heads_dev
    state = sbuf.shape[3] // 2
    half = n // 2

    barrier = pltpu.get_barrier_semaphore()

    def greet_buf(j, carry):
        pl.semaphore_signal(barrier, inc=1, device_id={"buf": lax.rem(me + j, n)}, device_id_type=MESH)
        return carry

    def greet_seq(j, carry):
        pl.semaphore_signal(barrier, inc=1, device_id={"seq": lax.rem(sq + j, ns)}, device_id_type=MESH)
        return carry

    lax.fori_loop(1, n, greet_buf, 0)
    lax.fori_loop(1, ns, greet_seq, 0)

    own_x = pltpu.make_async_copy(
        inputs_ref.at[:, :, pl.ds(pl.multiple_of(me * width, width), width)], xbuf.at[0], own_sem.at[0])
    own_s = pltpu.make_async_copy(shared_ref, sbuf.at[0], own_sem.at[1])
    own_x.start()
    own_s.start()

    step_out[...] = jnp.zeros_like(step_out)
    for b in range(buffers):
        turned = steps_ref[b].astype(jnp.float32).T
        for g in range(n):
            step_out[g, b * heads_dev:(b + 1) * heads_dev, :] = turned[g * heads_dev:(g + 1) * heads_dev, :]
    count = count_ref[0]
    row_id = lax.broadcasted_iota(jnp.int32, meta_out.shape, 0)
    meta = jnp.full(meta_out.shape, stream_rows, jnp.int32)
    for b in range(buffers):
        slot = jnp.clip(slot_ref[b] - sq * stream_rows, 0, stream_rows - 1)
        meta = jnp.where(row_id == b, jnp.where(b < count, slot, stream_rows), meta)
    meta_out[...] = meta
    meta_in[0] = meta
    step_in[0] = step_out[me]

    pl.semaphore_wait(barrier, n - 1 + ns - 1)

    def x_copy(j):
        peer = lax.rem(me + j, n)
        return pltpu.make_async_remote_copy(
            src_ref=inputs_ref.at[:, :, pl.ds(pl.multiple_of(peer * width, width), width)],
            dst_ref=xbuf.at[j], send_sem=x_send.at[j], recv_sem=x_recv.at[j],
            device_id={"buf": peer}, device_id_type=MESH)

    def step_copy(j):
        peer = lax.rem(me + j, n)
        return pltpu.make_async_remote_copy(
            src_ref=step_out.at[peer], dst_ref=step_in.at[j], send_sem=st_send.at[j], recv_sem=st_recv.at[j],
            device_id={"buf": peer}, device_id_type=MESH)

    def meta_copy(j):
        peer = lax.rem(me + j, n)
        return pltpu.make_async_remote_copy(
            src_ref=meta_out, dst_ref=meta_in.at[j], send_sem=m_send.at[j], recv_sem=m_recv.at[j],
            device_id={"buf": peer}, device_id_type=MESH)

    def shared_copy(i):
        peer = lax.rem(me + 2 * i, n)
        return pltpu.make_async_remote_copy(
            src_ref=shared_ref, dst_ref=sbuf.at[2 * i], send_sem=s_send.at[i], recv_sem=s_recv.at[2 * i],
            device_id={"buf": peer}, device_id_type=MESH)

    def forward_copy(i, src):
        slot = lax.rem(2 * i + 1 - 2 * bit + n, n)
        return pltpu.make_async_remote_copy(
            src_ref=src, dst_ref=sbuf.at[slot], send_sem=f_send.at[i], recv_sem=s_recv.at[slot],
            device_id={"buf": partner}, device_id_type=MESH)

    def shared_arrival(j):
        return pltpu.make_async_remote_copy(
            src_ref=shared_ref, dst_ref=sbuf.at[j], send_sem=f_send.at[0], recv_sem=s_recv.at[j],
            device_id={"buf": partner}, device_id_type=MESH)

    def leave_copy(i):
        return pltpu.make_async_remote_copy(
            src_ref=leave_out, dst_ref=leave_in.at[i], send_sem=l_send.at[i], recv_sem=l_recv.at[i],
            device_id={"seq": lax.rem(sq + i, ns)}, device_id_type=MESH)

    def start_small(j, carry):
        meta_copy(j).start()
        step_copy(j).start()
        return carry

    def start_shared(i, carry):
        shared_copy(i).start()
        return carry

    def start_x(j, carry):
        x_copy(j).start()
        return carry

    lax.fori_loop(1, n, start_small, 0)
    lax.fori_loop(1, half, start_shared, 0)
    forward_copy(0, shared_ref).start()
    lax.fori_loop(1, n, start_x, 0)

    def wait_small(j, carry):
        meta_copy(j).wait_recv()
        step_copy(j).wait_recv()
        return carry

    lax.fori_loop(1, n, wait_small, 0)
    to_scalar = pltpu.make_async_copy(meta_in, meta_smem, own_sem.at[2])
    to_scalar.start()

    shape = (n * 8, row_len)
    tri_up = (lax.broadcasted_iota(jnp.int32, (row_len, row_len), 0)
              <= lax.broadcasted_iota(jnp.int32, (row_len, row_len), 1)).astype(jnp.float32)
    head_row = lax.rem(lax.broadcasted_iota(jnp.int32, shape, 0), heads_dev)
    bias = jnp.full(shape, bias_ref[0], jnp.float32)
    decay = jnp.full(shape, log_ref[0], jnp.float32)
    for h in range(1, heads_dev):
        bias = jnp.where(head_row == h, bias_ref[h], bias)
        decay = jnp.where(head_row == h, log_ref[h], decay)
    step = softplus(step_in[...].reshape(shape) + bias)
    cum = jnp.dot(-step * jnp.exp(decay), tri_up, precision=EXACT, preferred_element_type=jnp.float32)

    to_scalar.wait()
    docs[...] = jnp.zeros_like(docs)

    def put_docs(j, carry):
        for b in range(buffers):
            slot = jnp.minimum(meta_smem[j, b, 0], stream_rows - 1)
            line = doc_ref[pl.ds(slot, 1), :].astype(jnp.float32)
            docs[j, b * heads_dev:(b + 1) * heads_dev, :] = jnp.broadcast_to(line, (heads_dev, row_len))
        return carry

    lax.fori_loop(0, n, put_docs, 0)

    def put_source(k, carry):
        found = jnp.int32(0)
        for j in range(n):
            for b in range(buffers):
                found = found + jnp.where(meta_smem[j, b, 0] == k, j * buffers + b, 0)
        source[k] = found
        return carry

    lax.fori_loop(0, stream_rows, put_source, 0)

    resets = jnp.dot(docs[...].reshape(shape), tri_up, precision=EXACT, preferred_element_type=jnp.float32)
    last_cum = cum[:, row_len - 1:row_len]
    last_resets = resets[:, row_len - 1:row_len]
    cube = (n, 8, row_len)
    cums[...] = cum.reshape(cube)
    counts_in[...] = resets.reshape(cube)
    steps_q[...] = step.reshape(cube)
    enters[...] = jnp.where(resets == 0.0, jnp.exp(cum), 0.0).reshape(cube)
    tails[...] = (jnp.where(resets == last_resets, jnp.exp(last_cum - cum), 0.0) * step).reshape(cube)
    passes[...] = jnp.broadcast_to(
        jnp.where(last_resets == 0.0, jnp.exp(last_cum), 0.0), shape).reshape(cube)

    own_s.wait()

    def pass_on(i, carry):
        shared_arrival(2 * i).wait_recv()
        forward_copy(i, sbuf.at[2 * i]).start()
        return carry

    lax.fori_loop(1, half, pass_on, 0)
    own_x.wait()

    lower = (lax.broadcasted_iota(jnp.int32, (row_len, row_len), 0)
             >= lax.broadcasted_iota(jnp.int32, (row_len, row_len), 1))
    lane_head = lax.broadcasted_iota(jnp.int32, (1, width), 1) // head_size
    gain = jnp.full((1, width), gain_ref[0], jnp.float32)
    for h in range(1, heads_dev):
        gain = jnp.where(lane_head == h, gain_ref[h], gain)

    def by_head(parts):
        full = jnp.broadcast_to(parts[0], (parts[0].shape[0], width))
        for h in range(1, heads_dev):
            full = jnp.where(lane_head == h, parts[h], full)
        return full

    def do_peer(j):
        cum_j = cums[j]
        resets_j = counts_in[j]
        step_j = steps_q[j]
        pass_j = passes[j]
        turned = jnp.concatenate([cum_j, resets_j, enters[j], tails[j]], axis=0).T
        for b in range(buffers):
            r = j * buffers + b
            x = xbuf[j, b]
            wide = x.astype(jnp.float32)
            b_part = sbuf[j, b, :, :state]
            c_part = sbuf[j, b, :, state:]
            scores = lax.dot_general(c_part, b_part, (((1,), (1,)), ((), ())),
                                     preferred_element_type=jnp.float32)
            q = b * heads_dev
            together = lower & (turned[:, 8 + q:9 + q] == resets_j[q:q + 1, :])
            weights = []
            masked = []
            for h in range(heads_dev):
                gap = turned[:, q + h:q + h + 1] - cum_j[q + h:q + h + 1, :]
                factor = jnp.exp(jnp.where(together, gap, -1e30))
                weights.append((scores * factor * step_j[q + h:q + h + 1, :]).astype(jnp.bfloat16))
                masked.append(jnp.where(lane_head == h, wide, 0.0).astype(jnp.bfloat16))
            within = jnp.dot(jnp.concatenate(weights, axis=1), jnp.concatenate(masked, axis=0),
                             preferred_element_type=jnp.float32)
            ybuf[r] = within + gain * wide
            ebuf[r] = by_head([turned[:, 16 + q + h:17 + q + h] for h in range(heads_dev)])
            tail = by_head([turned[:, 24 + q + h:25 + q + h] for h in range(heads_dev)])
            weighted = (wide * tail).astype(jnp.bfloat16)
            span_state[r] = lax.dot_general(b_part, weighted, (((0,), (0,)), ((), ())),
                                            preferred_element_type=jnp.float32)
            row_pass[r] = jnp.broadcast_to(by_head([pass_j[q + h:q + h + 1, :] for h in range(heads_dev)]),
                                           (8, width))

    do_peer(0)

    def arrive_odd_even(i, carry):
        j = 2 * i + 1
        x_copy(j).wait_recv()
        shared_arrival(j).wait_recv()
        do_peer(j)
        return carry

    def arrive_even(i, carry):
        x_copy(2 * i).wait_recv()
        do_peer(2 * i)
        return carry

    lax.fori_loop(1, half, arrive_even, 0)
    lax.fori_loop(0, half, arrive_odd_even, 0)

    def chain(k, carry):
        st, prod = carry
        r = source[k]
        incoming[k] = st
        prior_pass[k] = prod
        pass_r = row_pass[r]
        return pass_r[0:1] * st + span_state[r], prod * pass_r

    st, prod = lax.fori_loop(
        0, stream_rows, chain,
        (jnp.zeros((state, width), jnp.float32), jnp.ones((8, width), jnp.float32)))
    leave_out[0:state, :] = st
    leave_out[state:state + 8, :] = prod

    def start_leave(i, carry):
        leave_copy(i).start()
        return carry

    lax.fori_loop(1, ns, start_leave, 0)

    def wait_leave(i, carry):
        leave_copy(i).wait_recv()
        return carry

    lax.fori_loop(1, ns, wait_leave, 0)

    def enter(i, state_in):
        back = ns - 1 - i
        message = leave_in[back]
        following = message[state:state + 1, :] * state_in + message[0:state, :]
        return jnp.where(sq >= back, following, state_in)

    entering = lax.fori_loop(0, ns - 1, enter, jnp.zeros((state, width), jnp.float32))

    def finish(k, carry):
        r = source[k]
        carried = (incoming[k] + prior_pass[k][0:1] * entering).astype(jnp.bfloat16)
        c_part = shared_row(r)[:, state:]
        from_state = jnp.dot(c_part, carried, preferred_element_type=jnp.float32)
        out_ref[pl.ds(pl.multiple_of(k * row_len, row_len), row_len), :] = (
            ybuf[r] + from_state * ebuf[r]).astype(out_ref.dtype)
        return carry

    def shared_row(r):
        return sbuf[r // buffers, lax.rem(r, buffers)]

    lax.fori_loop(0, stream_rows, finish, 0)

    def end_buf(j, carry):
        x_copy(j).wait_send()
        step_copy(j).wait_send()
        meta_copy(j).wait_send()
        return carry

    def end_shared(i, carry):
        shared_copy(i).wait_send()
        forward_copy(i, sbuf.at[2 * i]).wait_send()
        return carry

    def end_leave(i, carry):
        leave_copy(i).wait_send()
        return carry

    lax.fori_loop(1, n, end_buf, 0)
    forward_copy(0, shared_ref).wait_send()
    lax.fori_loop(1, half, end_shared, 0)
    lax.fori_loop(1, ns, end_leave, 0)


def per_device(n, ns, row_inputs, row_shared, row_steps, row_count, row_slot, doc_start,
               decay_log, step_bias, skip_gain):
    buffers, row_len, inner = row_inputs.shape
    heads_dev = decay_log.shape[0]
    width = inner // n
    cols = row_shared.shape[2]
    state = cols // 2
    tokens = doc_start.shape[0]
    stream_rows = tokens // row_len
    total = n * buffers
    vmem = pl.BlockSpec(memory_space=pltpu.VMEM)
    smem = pl.BlockSpec(memory_space=pltpu.SMEM)
    hbm = pl.BlockSpec(memory_space=pl.ANY)
    f32, bf16, i32 = jnp.float32, jnp.bfloat16, jnp.int32
    dma = pltpu.SemaphoreType.DMA
    return pl.pallas_call(
        functools.partial(kernel, n, ns, heads_dev, stream_rows),
        out_shape=jax.ShapeDtypeStruct((tokens, width), bf16),
        in_specs=[hbm, hbm, vmem, smem, smem, vmem, smem, smem, smem],
        out_specs=vmem,
        scratch_shapes=[
            pltpu.VMEM((n, buffers, row_len, width), bf16),
            pltpu.VMEM((n, buffers, row_len, cols), bf16),
            pltpu.VMEM((n, 8, row_len), f32),
            pltpu.VMEM((n, 8, row_len), f32),
            pltpu.VMEM((8, 128), i32),
            pltpu.VMEM((n, 8, 128), i32),
            pltpu.SMEM((n, 8, 128), i32),
            pltpu.SMEM((stream_rows,), i32),
        ] + [pltpu.VMEM((n, 8, row_len), f32)] * 7 + [
            pltpu.VMEM((total, row_len, width), f32),
            pltpu.VMEM((total, row_len, width), f32),
            pltpu.VMEM((total, state, width), f32),
            pltpu.VMEM((total, 8, width), f32),
            pltpu.VMEM((stream_rows, state, width), f32),
            pltpu.VMEM((stream_rows, 8, width), f32),
            pltpu.VMEM((state + 8, width), f32),
            pltpu.VMEM((ns, state + 8, width), f32),
            dma((n,)), dma((n,)), dma((n,)), dma((n,)), dma((n,)),
            dma((n,)), dma((n,)), dma((n,)), dma((n,)), dma((ns,)), dma((ns,)), dma((3,)),
        ],
        compiler_params=pltpu.CompilerParams(
            collective_id=0, has_side_effects=True, vmem_limit_bytes=40 * 1024 * 1024),
    )(row_inputs, row_shared, row_steps, row_count, row_slot,
      doc_start.reshape(stream_rows, row_len), decay_log, step_bias, skip_gain)


def solution(mesh):
    return jax.shard_map(
        functools.partial(per_device, mesh.shape["buf"], mesh.shape["seq"]),
        mesh=mesh,
        in_specs=(
            P(("seq", "buf"), None, None),
            P(("seq", "buf"), None, None),
            P(("seq", "buf"), None, None),
            P(("seq", "buf")),
            P(("seq", "buf")),
            P("seq"),
            P("buf"),
            P("buf"),
            P("buf"),
        ),
        out_specs=P("seq", "buf"),
        check_vma=False,
    )
```

time: 94.9 us -> 36.8 us (0.39)
  the two profiles are of different devices: /device:TPU:1 before, /device:TPU:25 now
where the time goes in v1:
time: 36.8 us; the launch traced here: 36.6 us
  Pallas kernels  33.2 us (90%)
  local copies, waits for them, and re-layouts  2.66 us (7%)
  between operations  0.78 us (2%)
    pallas_call x1, Pallas kernels, per_device(): pl.pallas_call(functools.partial(kernel, n, ns, heads_dev, stream_rows),...  33.2 us
    unnamed x16, local copies, waits for them, and re-layouts  2.66 us

profile of v1, /device:TPU:25, one launch (start us, length us, event | category | flops | bytes accessed | tf_op | source)
XLA Modules:
  0.0 36.6 jit_solution(3219991477113240441)
XLA Ops:
  0.0 0.0 copy-start.1
  0.7 0.0 copy-start.2
  0.7 0.0 copy-start.3
  0.7 0.0 copy-start.4
  0.7 0.0 copy-start.5
  0.7 0.0 copy-start.6
  0.7 0.8 %copy.10.steps_ref = bf16[2,128,16]{2,1,0:T(8,128)(2,1)S(1)} copy(bf16[2,128,16]{1,2,0:T(8,128)(2,1)} %param.11) | data formatting | bytes 16384 | tf_op args[2]
  1.6 0.0 copy-done.1
  1.6 0.0 copy-done.2
  1.6 0.0 copy-done.3
  1.6 0.0 copy-done.4
  1.6 0.0 copy-done.5
  1.6 0.0 copy-done.6
  1.6 0.0 copy-start
  1.6 1.0 %copy-done = bf16[2,128,1024]{2,1,0:T(8,128)(2,1)S(1)} copy-done((bf16[2,128,1024]{2,1,0:T(8,128)(2,1)S(1)}, bf16[2,128,1024]{2,1,0:T(8,128)(2,1)}, u32[]{:S(2)}) %copy-start) | copy-done | bytes 524312
  2.7 33.2 %shard_map.91 = bf16[1536,128]{1,0:T(8,128)(2,1)S(1)} custom-call(bf16[2,128,1024]{2,1,0:T(8,128)(2,1)S(1)} %copy-done, bf16[2,128,128]{2,1,0:T(8,128)(2,1)S(1)} %copy-done.1, bf16[2,128,16]{2,1,0:T(8,128)(2,1)S(1)} %copy.10.steps_ref, s32[1]{0:T(128)S(6)} %copy.12.count_ref, s32[2]{0:T(128)S(1)} %copy-done.3, s32[12,128]{1,0:T(8,128)S(1)} %bitcast.1, ...), custom_call_target="tpu_custom_call" | custom-call | tf_op jit(solution)/shard_map/pallas_call | solution.py:351
  35.9 0.7 %copy.13 = bf16[1536,128]{1,0:T(8,128)(2,1)} copy(bf16[1536,128]{1,0:T(8,128)(2,1)S(1)} %shard_map.91) | data formatting | bytes 786432
Async XLA Ops:
  0.0 1.6 %copy-start.1 = (bf16[2,128,128]{2,1,0:T(8,128)(2,1)S(1)}, bf16[2,128,128]{2,1,0:T(8,128)(2,1)}, u32[]{:S(2)}) copy-start(bf16[2,128,128]{2,1,0:T(8,128)(2,1)} %shared_ref.1) | copy-start | bytes 196612
  0.7 0.9 %copy-start.2 = (s32[1536]{0:T(1024)S(1)}, s32[1536]{0:T(1024)}, u32[]{:S(2)}) copy-start(s32[1536]{0:T(1024)} %param.14) | copy-start | bytes 18436
  0.7 0.9 %copy-start.3 = (s32[2]{0:T(128)S(1)}, s32[2]{0:T(128)}, u32[]{:S(2)}) copy-start(s32[2]{0:T(128)} %slot_ref.1) | copy-start | bytes 28
  0.7 0.9 %copy-start.4 = (f32[2]{0:T(128)S(1)}, f32[2]{0:T(128)}, u32[]{:S(2)}) copy-start(f32[2]{0:T(128)} %log_ref.1) | copy-start | bytes 28
  0.7 0.9 %copy-start.5 = (f32[2]{0:T(128)S(1)}, f32[2]{0:T(128)}, u32[]{:S(2)}) copy-start(f32[2]{0:T(128)} %bias_ref.1) | copy-start | bytes 28
  0.7 0.9 %copy-start.6 = (f32[2]{0:T(128)S(1)}, f32[2]{0:T(128)}, u32[]{:S(2)}) copy-start(f32[2]{0:T(128)} %gain_ref.1) | copy-start | bytes 28
  1.6 1.0 %copy-start = (bf16[2,128,1024]{2,1,0:T(8,128)(2,1)S(1)}, bf16[2,128,1024]{2,1,0:T(8,128)(2,1)}, u32[]{:S(2)}) copy-start(bf16[2,128,1024]{2,1,0:T(8,128)(2,1)} %inputs_ref.1) | copy-start | bytes 1572868

commit v2 on v1

--- a/solution.py
+++ b/solution.py
@@ -34,7 +34,7 @@
     sq = lax.axis_index("seq")
     bit = lax.rem(me, 2)
     partner = me + 1 - 2 * bit
-    buffers, row_len = steps_ref.shape[0], steps_ref.shape[1]
+    buffers, row_len = steps_ref.shape[0], steps_ref.shape[2]
     width = xbuf.shape[3]
     head_size = width // heads_dev
     state = sbuf.shape[3] // 2
@@ -61,11 +61,11 @@
 
     step_out[...] = jnp.zeros_like(step_out)
     for b in range(buffers):
-        turned = steps_ref[b].astype(jnp.float32).T
+        turned = steps_ref[b].astype(jnp.float32)
         for g in range(n):
             step_out[g, b * heads_dev:(b + 1) * heads_dev, :] = turned[g * heads_dev:(g + 1) * heads_dev, :]
     count = count_ref[0]
-    row_id = lax.broadcasted_iota(jnp.int32, meta_out.shape, 0)
+    row_id = lax.broadcasted_iota(jnp.int32, meta_out.shape, 1)
     meta = jnp.full(meta_out.shape, stream_rows, jnp.int32)
     for b in range(buffers):
         slot = jnp.clip(slot_ref[b] - sq * stream_rows, 0, stream_rows - 1)
@@ -133,7 +133,8 @@
     lax.fori_loop(1, n, start_small, 0)
     lax.fori_loop(1, half, start_shared, 0)
     forward_copy(0, shared_ref).start()
-    lax.fori_loop(1, n, start_x, 0)
+    lax.fori_loop(1, half, lambda i, c: start_x(2 * i, c), 0)
+    lax.fori_loop(0, half, lambda i, c: start_x(2 * i + 1, c), 0)
 
     def wait_small(j, carry):
         meta_copy(j).wait_recv()
@@ -143,6 +144,13 @@
     lax.fori_loop(1, n, wait_small, 0)
     to_scalar = pltpu.make_async_copy(meta_in, meta_smem, own_sem.at[2])
     to_scalar.start()
+
+    def pass_on(i, carry):
+        shared_arrival(2 * i).wait_recv()
+        forward_copy(i, sbuf.at[2 * i]).start()
+        return carry
+
+    lax.fori_loop(1, half, pass_on, 0)
 
     shape = (n * 8, row_len)
     tri_up = (lax.broadcasted_iota(jnp.int32, (row_len, row_len), 0)
@@ -161,7 +169,7 @@
 
     def put_docs(j, carry):
         for b in range(buffers):
-            slot = jnp.minimum(meta_smem[j, b, 0], stream_rows - 1)
+            slot = jnp.minimum(meta_smem[j, 0, b], stream_rows - 1)
             line = doc_ref[pl.ds(slot, 1), :].astype(jnp.float32)
             docs[j, b * heads_dev:(b + 1) * heads_dev, :] = jnp.broadcast_to(line, (heads_dev, row_len))
         return carry
@@ -172,7 +180,7 @@
         found = jnp.int32(0)
         for j in range(n):
             for b in range(buffers):
-                found = found + jnp.where(meta_smem[j, b, 0] == k, j * buffers + b, 0)
+                found = found + jnp.where(meta_smem[j, 0, b] == k, j * buffers + b, 0)
         source[k] = found
         return carry
 
@@ -191,13 +199,6 @@
         jnp.where(last_resets == 0.0, jnp.exp(last_cum), 0.0), shape).reshape(cube)
 
     own_s.wait()
-
-    def pass_on(i, carry):
-        shared_arrival(2 * i).wait_recv()
-        forward_copy(i, sbuf.at[2 * i]).start()
-        return carry
-
-    lax.fori_loop(1, half, pass_on, 0)
     own_x.wait()
 
     lower = (lax.broadcasted_iota(jnp.int32, (row_len, row_len), 0)
@@ -272,8 +273,13 @@
         pass_r = row_pass[r]
         return pass_r[0:1] * st + span_state[r], prod * pass_r
 
+    def chain_some(i, carry):
+        for u in range(6):
+            carry = chain(6 * i + u, carry)
+        return carry
+
     st, prod = lax.fori_loop(
-        0, stream_rows, chain,
+        0, stream_rows // 6, chain_some,
         (jnp.zeros((state, width), jnp.float32), jnp.ones((8, width), jnp.float32)))
     leave_out[0:state, :] = st
     leave_out[state:state + 8, :] = prod
@@ -282,21 +288,21 @@
         leave_copy(i).start()
         return carry
 
-    lax.fori_loop(1, ns, start_leave, 0)
+    lax.fori_loop(1, ns - sq, start_leave, 0)
 
     def wait_leave(i, carry):
         leave_copy(i).wait_recv()
         return carry
 
-    lax.fori_loop(1, ns, wait_leave, 0)
+    lax.fori_loop(1, sq + 1, wait_leave, 0)
 
     def enter(i, state_in):
-        back = ns - 1 - i
+        back = sq - i
         message = leave_in[back]
         following = message[state:state + 1, :] * state_in + message[0:state, :]
-        return jnp.where(sq >= back, following, state_in)
-
-    entering = lax.fori_loop(0, ns - 1, enter, jnp.zeros((state, width), jnp.float32))
+        return following
+
+    entering = lax.fori_loop(0, sq, enter, jnp.zeros((state, width), jnp.float32))
 
     def finish(k, carry):
         r = source[k]
@@ -310,7 +316,12 @@
     def shared_row(r):
         return sbuf[r // buffers, lax.rem(r, buffers)]
 
-    lax.fori_loop(0, stream_rows, finish, 0)
+    def finish_some(i, carry):
+        for u in range(6):
+            finish(6 * i + u, 0)
+        return carry
+
+    lax.fori_loop(0, stream_rows // 6, finish_some, 0)
 
     def end_buf(j, carry):
         x_copy(j).wait_send()
@@ -330,7 +341,7 @@
     lax.fori_loop(1, n, end_buf, 0)
     forward_copy(0, shared_ref).wait_send()
     lax.fori_loop(1, half, end_shared, 0)
-    lax.fori_loop(1, ns, end_leave, 0)
+    lax.fori_loop(1, ns - sq, end_leave, 0)
 
 
 def per_device(n, ns, row_inputs, row_shared, row_steps, row_count, row_slot, doc_start,
@@ -358,9 +369,9 @@
             pltpu.VMEM((n, buffers, row_len, cols), bf16),
             pltpu.VMEM((n, 8, row_len), f32),
             pltpu.VMEM((n, 8, row_len), f32),
-            pltpu.VMEM((8, 128), i32),
-            pltpu.VMEM((n, 8, 128), i32),
-            pltpu.SMEM((n, 8, 128), i32),
+            pltpu.VMEM((1, 128), i32),
+            pltpu.VMEM((n, 1, 128), i32),
+            pltpu.SMEM((n, 1, 128), i32),
             pltpu.SMEM((stream_rows,), i32),
         ] + [pltpu.VMEM((n, 8, row_len), f32)] * 7 + [
             pltpu.VMEM((total, row_len, width), f32),
@@ -375,8 +386,8 @@
             dma((n,)), dma((n,)), dma((n,)), dma((n,)), dma((ns,)), dma((ns,)), dma((3,)),
         ],
         compiler_params=pltpu.CompilerParams(
-            collective_id=0, has_side_effects=True, vmem_limit_bytes=40 * 1024 * 1024),
-    )(row_inputs, row_shared, row_steps, row_count, row_slot,
+            collective_id=0, has_side_effects=True, vmem_limit_bytes=60 * 1024 * 1024),
+    )(row_inputs, row_shared, row_steps.transpose(0, 2, 1), row_count, row_slot,
       doc_start.reshape(stream_rows, row_len), decay_log, step_bias, skip_gain)
 
 

time: 36.8 us -> 33.2 us (0.902)
  the two profiles are of different devices: /device:TPU:25 before, /device:TPU:5 now
where the time goes in v2:
time: 33.2 us; the launch traced here: 33 us
  Pallas kernels  30.5 us (92%)
  local copies, waits for them, and re-layouts  1.77 us (5%)
  between operations  0.66 us (2%)
    pallas_call x1, Pallas kernels, per_device(): pl.pallas_call(functools.partial(kernel, n, ns, heads_dev, stream_rows),...  30.5 us
    unnamed x1, local copies, waits for them, and re-layouts  1.77 us

profile of v2, /device:TPU:5, one launch (start us, length us, event | category | flops | bytes accessed | tf_op | source)
XLA Modules:
  0.0 33.0 jit_solution(4835799232515622134)
XLA Ops:
  0.7 30.5 %shard_map.91 = bf16[1536,128]{1,0:T(8,128)(2,1)} custom-call(bf16[2,128,1024]{2,1,0:T(8,128)(2,1)} %inputs_ref.1, bf16[2,128,128]{2,1,0:T(8,128)(2,1)} %shared_ref.1, bf16[2,16,128]{2,1,0:T(8,128)(2,1)} %bitcast.2, s32[1]{0:T(128)S(6)} %copy.11.count_ref, s32[2]{0:T(128)} %slot_ref.1, s32[12,128]{1,0:T(8,128)} %bitcast.3, f32[2]{0:T(128)} %log_ref.1, ...), custom_call_target="tpu_custom_call" | custom-call | tf_op jit(solution)/shard_map/pallas_call | solution.py:362
  31.2 1.8 %copy.12 = bf16[1536,128]{1,0:T(8,128)(2,1)} copy(bf16[1536,128]{1,0:T(8,128)(2,1)} %shard_map.91) | data formatting | bytes 786432

commit v3 on v2

--- a/solution.py
+++ b/solution.py
@@ -24,8 +24,8 @@
 def kernel(
     n, ns, heads_dev, stream_rows,
     inputs_ref, shared_ref, steps_ref, count_ref, slot_ref, doc_ref, log_ref, bias_ref, gain_ref,
-    out_ref,
-    xbuf, sbuf, step_out, step_in, meta_out, meta_in, meta_smem, source,
+    result_ref,
+    out_ref, out_sem, xbuf, sbuf, step_out, step_in, meta_out, meta_in, meta_smem, source,
     docs, cums, counts_in, steps_q, enters, tails, passes,
     ybuf, ebuf, span_state, row_pass, incoming, prior_pass, leave_out, leave_in,
     x_send, x_recv, s_send, s_recv, f_send, st_send, st_recv, m_send, m_recv, l_send, l_recv, own_sem,
@@ -133,8 +133,7 @@
     lax.fori_loop(1, n, start_small, 0)
     lax.fori_loop(1, half, start_shared, 0)
     forward_copy(0, shared_ref).start()
-    lax.fori_loop(1, half, lambda i, c: start_x(2 * i, c), 0)
-    lax.fori_loop(0, half, lambda i, c: start_x(2 * i + 1, c), 0)
+    lax.fori_loop(1, n, start_x, 0)
 
     def wait_small(j, carry):
         meta_copy(j).wait_recv()
@@ -316,9 +315,18 @@
     def shared_row(r):
         return sbuf[r // buffers, lax.rem(r, buffers)]
 
+    def out_copy(i):
+        part = pl.ds(pl.multiple_of(i * 6 * row_len, row_len), 6 * row_len)
+        return pltpu.make_async_copy(out_ref.at[part, :], result_ref.at[part, :], out_sem.at[i])
+
+    def end_out(i, carry):
+        out_copy(i).wait()
+        return carry
+
     def finish_some(i, carry):
         for u in range(6):
             finish(6 * i + u, 0)
+        out_copy(i).start()
         return carry
 
     lax.fori_loop(0, stream_rows // 6, finish_some, 0)
@@ -339,6 +347,7 @@
         return carry
 
     lax.fori_loop(1, n, end_buf, 0)
+    lax.fori_loop(0, stream_rows // 6, end_out, 0)
     forward_copy(0, shared_ref).wait_send()
     lax.fori_loop(1, half, end_shared, 0)
     lax.fori_loop(1, ns - sq, end_leave, 0)
@@ -363,8 +372,10 @@
         functools.partial(kernel, n, ns, heads_dev, stream_rows),
         out_shape=jax.ShapeDtypeStruct((tokens, width), bf16),
         in_specs=[hbm, hbm, vmem, smem, smem, vmem, smem, smem, smem],
-        out_specs=vmem,
+        out_specs=hbm,
         scratch_shapes=[
+            pltpu.VMEM((tokens, width), bf16),
+            dma((stream_rows // 6,)),
             pltpu.VMEM((n, buffers, row_len, width), bf16),
             pltpu.VMEM((n, buffers, row_len, cols), bf16),
             pltpu.VMEM((n, 8, row_len), f32),

time: 33.2 us -> 33.2 us (level)
  the two profiles are of different devices: /device:TPU:5 before, /device:TPU:15 now
where the time goes in v3:
time: 33.2 us; the launch traced here: 33 us
  Pallas kernels  30.6 us (92%)
  local copies, waits for them, and re-layouts  1.77 us (5%)
  between operations  0.66 us (2%)
    pallas_call x1, Pallas kernels, per_device(): pl.pallas_call(functools.partial(kernel, n, ns, heads_dev, stream_rows),...  30.6 us
    unnamed x1, local copies, waits for them, and re-layouts  1.77 us

profile of v3, /device:TPU:15, one launch (start us, length us, event | category | flops | bytes accessed | tf_op | source)
XLA Modules:
  0.0 33.0 jit_solution(12901724941534913235)
XLA Ops:
  0.7 30.6 %shard_map.91 = bf16[1536,128]{1,0:T(8,128)(2,1)} custom-call(bf16[2,128,1024]{2,1,0:T(8,128)(2,1)} %inputs_ref.1, bf16[2,128,128]{2,1,0:T(8,128)(2,1)} %shared_ref.1, bf16[2,16,128]{2,1,0:T(8,128)(2,1)} %bitcast.2, s32[1]{0:T(128)S(6)} %copy.11.count_ref, s32[2]{0:T(128)} %slot_ref.1, s32[12,128]{1,0:T(8,128)} %bitcast.3, f32[2]{0:T(128)} %log_ref.1, ...), custom_call_target="tpu_custom_call" | custom-call | tf_op jit(solution)/shard_map/pallas_call | solution.py:371
  31.2 1.8 %copy.12 = bf16[1536,128]{1,0:T(8,128)(2,1)} copy(bf16[1536,128]{1,0:T(8,128)(2,1)} %shard_map.91) | data formatting | bytes 786432
